TPU v7x, 256 devices: a whole 4x4x8 slice. The times are simulated.
256 devices in a mesh: group: 8 (over z), member: 32 (over x, y, core).
Axes of the slice: x: 4, y: 4, z: 8, core: 2. Of those that a mesh axis runs over, the one named last changes fastest.
Arguments:
- object_tiles: float32 [2, 2, 4096, 16384], P(None, None, 'group', 'member'), may hold values from -1 to 1
- probe_modes: float32 [2, 2, 128, 128], replicated, may hold values from -6 to 6
- measured: float32 [8, 32, 8, 128, 128], P('group', 'member'), may hold values from 1 to 3
- slot_offset: int32 [8, 32, 8, 2], P('group', 'member'), may hold values from 0 to 511, as said below
- slot_count: int32 [8, 32], replicated, may hold values from 1 to 8, as said below
Outputs:
- object_grad: float32 [2, 2, 4096, 16384], P(None, None, 'group', 'member')
- probe_grad: float32 [2, 2, 128, 128], replicated
Inputs may be any that keep to these rules, and one draw needn't show every extreme that they name: Every draw has a device with 8 positions; only a device's first slot_count slots are positions. `slot_offset`: on the last tile row the row offsets are at most 384, on the last tile column the column offsets likewise, so every patch lies inside the object; elsewhere a patch may reach into the tiles to the right, below, and below right.
All inputs are finite; a program needn't handle non-finite values.
Results may differ from a plain program's by a relative error of at most 0.00011.
Values sent between devices are 32-bit elements; how exact they have to be, the bound alone decides.
A program may use at most 64 MiB of HBM per device.

v0:
```python
import math

import jax
import jax.numpy as jnp
from jax import lax
from jax.sharding import PartitionSpec as P

fresnel_rate = 0.5


def from_behind(block, axis, distance):
    devices = range(lax.axis_size(axis))
    route = [(i - distance, i) for i in devices if i - distance in devices]
    return lax.ppermute(block, axis, route)


def make_tables(size):
    freq = jnp.arange(size, dtype=jnp.int32)
    product = freq[:, None] * freq[None, :] % size
    angle = 2.0 * math.pi * product.astype(jnp.float32) / size
    norm_scale = 1.0 / math.sqrt(size)
    signed = jnp.where(freq >= size // 2, freq - size, freq).astype(jnp.float32)
    phase = -math.pi * fresnel_rate * (signed[:, None] ** 2 + signed[None, :] ** 2) / size
    return (
        jnp.cos(angle) * norm_scale,
        jnp.sin(angle) * norm_scale,
        jnp.cos(phase),
        jnp.sin(phase),
    )


def transform(real_part, imag_part, cos_table, sin_table, direction):
    highest = lax.Precision.HIGHEST

    def from_left(matrix, batch):
        return jnp.einsum("ij,bjk->bik", matrix, batch, precision=highest)

    def from_right(batch, matrix):
        return jnp.einsum("bij,jk->bik", batch, matrix, precision=highest)

    half_real = from_left(cos_table, real_part) + direction * from_left(sin_table, imag_part)
    half_imag = from_left(cos_table, imag_part) - direction * from_left(sin_table, real_part)
    full_real = from_right(half_real, cos_table) + direction * from_right(half_imag, sin_table)
    full_imag = from_right(half_imag, cos_table) - direction * from_right(half_real, sin_table)
    return (full_real, full_imag)


def position_loss(patch_cut, probe_modes, amplitude, tables):
    cos_table, sin_table, kernel_real, kernel_imag = tables
    wave_real = probe_modes[:, 0]
    wave_imag = probe_modes[:, 1]
    layers = patch_cut.shape[0]
    for layer_index in range(layers):
        obj_real = patch_cut[layer_index, 0]
        obj_imag = patch_cut[layer_index, 1]
        next_real = wave_real * obj_real - wave_imag * obj_imag
        next_imag = wave_real * obj_imag + wave_imag * obj_real
        if layer_index < layers - 1:
            spec_real, spec_imag = transform(next_real, next_imag, cos_table, sin_table, 1.0)
            prop_real = spec_real * kernel_real - spec_imag * kernel_imag
            prop_imag = spec_real * kernel_imag + spec_imag * kernel_real
            wave_real, wave_imag = transform(prop_real, prop_imag, cos_table, sin_table, -1.0)
        else:
            wave_real, wave_imag = (next_real, next_imag)
    far_real, far_imag = transform(wave_real, wave_imag, cos_table, sin_table, 1.0)
    intensity = jnp.sum(far_real * far_real + far_imag * far_imag, axis=0)
    return jnp.sum((jnp.sqrt(intensity + 1.0) - amplitude) ** 2)


def cut_patch(extended, row_start, col_start, patch_size):
    zero_index = jnp.int32(0)
    starts = (zero_index, zero_index, row_start, col_start)
    return lax.dynamic_slice(extended, starts, (extended.shape[0], 2, patch_size, patch_size))


def add_patch(grad_ext, update, row_start, col_start):
    zero_index = jnp.int32(0)
    starts = (zero_index, zero_index, row_start, col_start)
    current = lax.dynamic_slice(grad_ext, starts, update.shape)
    return lax.dynamic_update_slice(grad_ext, current + update, starts)


def per_device(object_tiles, probe_modes, measured, slot_offset, slot_count):
    layers, _, tile_rows, tile_cols = object_tiles.shape
    patch_size = probe_modes.shape[-1]
    capacity = measured.shape[2]
    offsets = slot_offset.reshape(capacity, 2)
    amplitudes = measured.reshape(capacity, patch_size, patch_size)
    group_index = lax.axis_index("group")
    member_index = lax.axis_index("member")
    own_count = slot_count[group_index, member_index]
    tables = make_tables(patch_size)
    gradient_fn = jax.grad(position_loss, argnums=(0, 1))
    right_rim = from_behind(object_tiles[:, :, :, :patch_size], "member", -1)
    widened = jnp.concatenate([object_tiles, right_rim], 3)
    lower_rim = from_behind(widened[:, :, :patch_size, :], "group", -1)
    extended = jnp.concatenate([widened, lower_rim], 2)
    grad_start = jnp.zeros(extended.shape, jnp.float32)
    probe_start = jnp.zeros(probe_modes.shape, jnp.float32)

    def own_step(item_index, carry):
        grad_ext, probe_acc = carry
        row_start = offsets[item_index, 0]
        col_start = offsets[item_index, 1]
        patch_cut = cut_patch(extended, row_start, col_start, patch_size)
        amplitude = lax.dynamic_index_in_dim(amplitudes, item_index, 0, keepdims=False)
        patch_grad, probe_part = gradient_fn(patch_cut, probe_modes, amplitude, tables)
        return (add_patch(grad_ext, patch_grad, row_start, col_start), probe_acc + probe_part)

    grad_ext, probe_acc = lax.fori_loop(0, own_count, own_step, (grad_start, probe_start))
    rows_home = from_behind(grad_ext[:, :, tile_rows:, :], "group", 1)
    grad_ext = grad_ext.at[:, :, :patch_size, :].add(rows_home)
    upper_part = grad_ext[:, :, :tile_rows, :]
    cols_home = from_behind(upper_part[:, :, :, tile_cols:], "member", 1)
    object_grad = upper_part[:, :, :, :tile_cols].at[:, :, :, :patch_size].add(cols_home)
    probe_total = lax.psum(probe_acc, ("group", "member"))
    total = jnp.sum(slot_count).astype(jnp.float32)
    return (object_grad, probe_total / jnp.sqrt(total))


def solution(mesh):
    placed = (
        P(None, None, "group", "member"),
        P(),
        P("group", "member", None, None, None),
        P("group", "member", None, None),
        P(),
    )
    return jax.shard_map(
        per_device,
        mesh=mesh,
        in_specs=placed,
        out_specs=(P(None, None, "group", "member"), P()),
        check_vma=False,
    )
```

profile of v0, /device:TPU:1, one launch (start us, length us, event | category | flops | bytes accessed | tf_op | source)
XLA Modules:
  0.0 695.5 jit_solution(4082180862791742156)
XLA Ops:
  7.2 1.3 slice.95
  8.5 5.3 collective-permute-start
  13.8 2.6 constant_dynamic-update-slice_fusion.1
  16.5 9.6 %collective-permute-done = f32[2,2,512,128]{3,2,1,0:T(8,128)S(1)} collective-permute-done((f32[2,2,512,128]{3,2,1,0:T(8,128)S(1)}, f32[2,2,512,128]{3,2,1,0:T(8,128)S(1)}, u32[]{:S(2)}, u32[]{:S(2)}) %collective-permute-start) | collective-permute-done | bytes 1048608 | tf_op jit(solution)/shard_map/ppermute | solution.py:14
  26.1 2.4 copy-done
  28.6 1.3 collective-permute-start.1
  30.0 0.6 dynamic_slice.19
  30.6 21.2 %collective-permute-done.1 = f32[2,2,128,640]{3,2,1,0:T(8,128)S(1)} collective-permute-done((f32[2,2,128,640]{3,2,1,0:T(8,128)S(1)}, f32[2,2,128,640]{3,2,1,0:T(8,128)S(1)}, u32[]{:S(2)}, u32[]{:S(2)}) %collective-permute-start.1) | collective-permute-done | bytes 1310752 | tf_op jit(solution)/shard_map/ppermute | solution.py:14
  51.9 5.7 pad_maximum_fusion
  57.5 3.1 broadcast_in_dim.10
  60.7 281.6 %while.17 = (s32[]{:T(128)}, f32[2,2,640,640]{3,2,1,0:T(8,128)}, f32[2,2,128,128]{2,3,0,1:T(8,128)S(1)}, s32[]{:T(128)}, s32[8,2]{0,1:T(2,128)S(1)}, /*index=5*/...) while((s32[]{:T(128)}, f32[2,2,640,640]{3,2,1,0:T(8,128)}, ...), condition=%wide.region_10.11_spmd.clone.clone.clone, body=%wide.region_0.10_spmd.clone.clone.clone.sunk | while | flops 2432663552 | bytes 27525928 | solution.py:110
  61.5 0.6 constant_dynamic-slice_fusion.3
  65.7 1.3 dynamic-slice_bitcast_fusion.5
  80.9 0.9 fusion.610
  94.3 0.6 add_bitcast_fusion.9
  95.4 1.2 add_add_fusion.4
  96.6 4.0 dynamic_update_slice.7
  101.3 0.6 constant_dynamic-slice_fusion.3
  105.5 1.3 dynamic-slice_bitcast_fusion.5
  120.7 0.9 fusion.610
  134.1 0.6 add_bitcast_fusion.9
  135.2 1.2 add_add_fusion.4
  136.4 4.4 dynamic_update_slice.7
  141.5 0.6 constant_dynamic-slice_fusion.3
  145.7 1.3 dynamic-slice_bitcast_fusion.5
  160.8 0.9 fusion.610
  174.3 0.6 add_bitcast_fusion.9
  175.4 1.2 add_add_fusion.4
  176.6 4.4 dynamic_update_slice.7
  181.7 0.6 constant_dynamic-slice_fusion.3
  185.8 1.3 dynamic-slice_bitcast_fusion.5
  201.0 0.9 fusion.610
  214.4 0.6 add_bitcast_fusion.9
  215.5 1.2 add_add_fusion.4
  216.8 4.3 dynamic_update_slice.7
  221.8 0.6 constant_dynamic-slice_fusion.3
  225.9 1.3 dynamic-slice_bitcast_fusion.5
  241.1 0.9 fusion.610
  255.7 1.2 add_add_fusion.4
  256.9 4.3 dynamic_update_slice.7
  261.9 0.6 constant_dynamic-slice_fusion.3
  266.0 1.3 dynamic-slice_bitcast_fusion.5
  281.2 0.9 fusion.610
  294.7 0.6 add_bitcast_fusion.9
  295.8 1.2 add_add_fusion.4
  297.0 4.2 dynamic_update_slice.7
  301.9 0.6 constant_dynamic-slice_fusion.3
  306.0 1.3 dynamic-slice_bitcast_fusion.5
  321.2 0.9 fusion.610
  335.8 1.2 add_add_fusion.4
  337.0 4.4 dynamic_update_slice.7
  342.2 1.4 slice.98
  343.7 1.4 collective-permute-start.2
  345.0 19.5 %collective-permute-done.2 = f32[2,2,128,640]{3,2,1,0:T(8,128)S(1)} collective-permute-done((f32[2,2,128,640]{3,2,1,0:T(8,128)S(1)}, f32[2,2,128,640]{3,2,1,0:T(8,128)S(1)}, u32[]{:S(2)}, u32[]{:S(2)}) %collective-permute-start.2) | collective-permute-done | bytes 1310752 | tf_op jit(solution)/shard_map/ppermute | solution.py:14
  364.6 2.6 add_dynamic-update-slice_fusion
  367.2 1.3 slice.123
  368.5 1.9 collective-permute-start.3
  370.4 0.8 copy.145
  371.3 0.6 reduce_sum.86
  372.6 308.2 %all-reduce.8.cloned.1.call-done = f32[2,2,128,128]{3,2,1,0:T(8,128)} async-done(((f32[2,2,128,128]{3,2,1,0:T(8,128)}), f32[2,2,128,128]{3,2,1,0:T(8,128)}) %all-reduce.8.cloned.1.call-update) | async-done | bytes 262160 | tf_op jit(solution)/shard_map/psum | solution.py:116
  680.8 1.7 broadcast_divide_fusion
  682.5 2.7 slice.121
  685.2 1.4 fusion.376
  686.6 2.0 copy-done.1
  (417 shorter events, 187.5 us)
Async XLA Ops:
  7.2 673.6 %all-reduce.8.cloned.1.call-start = ((), (), s32[]{:S(2)}) async-start(), calls=%async_computation | async-start | bytes 524288 | tf_op jit(solution)/shard_map/psum | solution.py:116
  8.5 21.4 %copy-start.2 = (f32[2,2,128,128]{3,2,1,0:T(8,128)S(1)}, f32[2,2,128,128]{3,2,1,0:T(8,128)}, u32[]{:S(2)}) copy-start(f32[2,2,128,128]{3,2,1,0:T(8,128)} %param.12) | copy-start | bytes 786436
  8.5 21.5 %copy-start.4 = (s32[8,32]{1,0:T(8,128)S(1)}, s32[8,32]{1,0:T(8,128)}, u32[]{:S(2)}) copy-start(s32[8,32]{1,0:T(8,128)} %param.15) | copy-start | bytes 3076
  8.5 17.5 %collective-permute-start = (f32[2,2,512,128]{3,2,1,0:T(8,128)S(1)}, f32[2,2,512,128]{3,2,1,0:T(8,128)S(1)}, u32[]{:S(2)}, u32[]{:S(2)}) collective-permute-start(f32[2,2,512,128]{3,2,1,0:T(8,128)S(1)} %slice.95), channel_id=1, source_target_pairs={{1,0},{2,1},{3,2},{4,3},{5,4},{6,5},{7,6},{8,7},{9,8},{10,9},{11,1... | collective-permute-start | bytes 3145736 | tf_op jit(solution)/shard_map/ppermute | solution.py:14
  26.1 2.4 copy-start
  28.6 23.3 %collective-permute-start.1 = (f32[2,2,128,640]{3,2,1,0:T(8,128)S(1)}, f32[2,2,128,640]{3,2,1,0:T(8,128)S(1)}, u32[]{:S(2)}, u32[]{:S(2)}) collective-permute-start(f32[2,2,128,640]{3,2,1,0:T(8,128)S(1)} %slice.120), channel_id=1, source_target_pairs={{32,0},{64,32},{96,64},{128,96},{160,128},{192,160},{224,192},{33,... | collective-permute-start | bytes 3932168 | tf_op jit(solution)/shard_map/ppermute | solution.py:14
  57.5 3.1 copy-start.3
  343.7 20.9 %collective-permute-start.2 = (f32[2,2,128,640]{3,2,1,0:T(8,128)S(1)}, f32[2,2,128,640]{3,2,1,0:T(8,128)S(1)}, u32[]{:S(2)}, u32[]{:S(2)}) collective-permute-start(f32[2,2,128,640]{3,2,1,0:T(8,128)S(1)} %slice.98), channel_id=1, source_target_pairs={{0,32},{32,64},{64,96},{96,128},{128,160},{160,192},{192,224},{1,3... | collective-permute-start | bytes 3932168 | tf_op jit(solution)/shard_map/ppermute | solution.py:14
  368.5 316.6 %collective-permute-start.3 = (f32[2,2,512,128]{3,2,1,0:T(8,128)S(1)}, f32[2,2,512,128]{3,2,1,0:T(8,128)S(1)}, u32[]{:S(2)}, u32[]{:S(2)}) collective-permute-start(f32[2,2,512,128]{3,2,1,0:T(8,128)S(1)} %slice.123), channel_id=1, source_target_pairs={{0,1},{1,2},{2,3},{3,4},{4,5},{5,6},{6,7},{7,8},{8,9},{9,10},{10,1... | collective-permute-start | bytes 3145736 | tf_op jit(solution)/shard_map/ppermute | solution.py:14
  686.6 2.0 copy-start.1
Sparse Core Ops, SparseCore 0:
  371.4 309.3 all-reduce.7
where the time goes:
time: 699 us; the launch traced here: 695 us
  waiting for transfers between devices  359 us (51%)
  matrix products  183 us (26%)
  local copies, waits for them, and re-layouts  65.6 us (9%)
  loops' own time  33.7 us (5%)
  other arithmetic  29.5 us (4%)
  between operations  14.9 us (2%)
  starting transfers between devices  9.9 us (1%)
    psum x1, waiting for transfers between devices, per_device(): probe_total = lax.psum(probe_acc, ('group', 'member'))  308 us
    dot_general x168, matrix products, from_left(): return jnp.einsum('ij,bjk->bik', matrix, batch, precision=highest)  92.9 us
    dot_general x168, matrix products, from_right(): return jnp.einsum('bij,jk->bik', batch, matrix, precision=highest)  90.3 us
    ppermute x4, waiting for transfers between devices, from_behind(): return lax.ppermute(block, axis, route)  50.3 us
    another operation x1, loops' own time, per_device(): lax.fori_loop(0, own_count, own_step, (grad_start, probe_start))  33.7 us
    dynamic_update_slice x7, local copies, waits for them, and re-layouts, add_patch(): return lax.dynamic_update_slice(grad_ext, current + update, starts)  30.1 us
  transfers between devices with their start and end apart: 5, of which 4 were waited for; matrix products, arithmetic and copies ran while one was open for 1% of the time, Pallas kernels for 0%

commit v1 on v0

v1 whole, which is shorter than its diff:
```python
import math

import jax
import jax.numpy as jnp
import ml_dtypes
import numpy as np
from jax import lax
from jax.experimental import pallas as pl
from jax.experimental.pallas import tpu as pltpu
from jax.sharding import PartitionSpec as P

MESH = pl.DeviceIdType.MESH
F32 = jnp.float32
BF16 = jnp.bfloat16
FRESNEL_RATE = 0.5
PAIR = 2


def make_tables(size):
    freq = np.arange(size)
    fourier = np.exp(-2j * np.pi * (np.outer(freq, freq) % size) / size) / math.sqrt(size)
    signed = np.where(freq >= size // 2, freq - size, freq).astype(np.float64)
    kernel = np.exp(-1j * np.pi * FRESNEL_RATE * signed**2 / size)
    spread = fourier.conj() @ (kernel[:, None] * fourier)
    spread = 0.5 * (spread + spread.T)
    forms = []
    for matrix in (fourier, spread):
        real, imag = matrix.real, matrix.imag
        forms.append(np.block([[real, -imag], [imag, real]]))
        forms.append(np.block([[real, imag], [-imag, real]]))
    exact = np.stack(forms)
    high = exact.astype(ml_dtypes.bfloat16)
    low = (exact - high.astype(np.float64)).astype(ml_dtypes.bfloat16)
    return np.stack([high, low], axis=1)


def split(x):
    high = x.astype(BF16)
    return high, (x - high.astype(F32)).astype(BF16)


def dot(a, b):
    return jnp.dot(a, b, preferred_element_type=F32)


def two_sided(tables, left, right, waves):
    size = waves[0][0].shape[0]
    x = jnp.concatenate(
        [jnp.concatenate([w[0] for w in waves], axis=1), jnp.concatenate([w[1] for w in waves], axis=1)], axis=0
    )
    high, low = split(x)
    t_high, t_low = tables[left, 0], tables[left, 1]
    t = dot(jnp.concatenate([t_high, t_high, t_low], axis=1), jnp.concatenate([high, low, high], axis=0))
    rows = []
    for j in range(len(waves)):
        cols = slice(j * size, (j + 1) * size)
        rows.append(jnp.concatenate([t[:size, cols], t[size:, cols]], axis=1))
    high, low = split(jnp.concatenate(rows, axis=0))
    t_high, t_low = tables[right, 0], tables[right, 1]
    y = dot(jnp.concatenate([high, low, high], axis=1), jnp.concatenate([t_high, t_high, t_low], axis=0))
    return [(y[j * size : (j + 1) * size, :size], y[j * size : (j + 1) * size, size:]) for j in range(len(waves))]


def times(a, b):
    return a[0] * b[0] - a[1] * b[1], a[0] * b[1] + a[1] * b[0]


def conj_times(a, b):
    return a[0] * b[0] + a[1] * b[1], a[0] * b[1] - a[1] * b[0]


def plus(a, b):
    return a[0] + b[0], a[1] + b[1]


def kernel(
    ng,
    nm,
    tile,
    size,
    cap,
    offset_ref,
    count_ref,
    counts_ref,
    object_ref,
    probe_ref,
    measured_ref,
    tables,
    grad_ref,
    probe_grad_ref,
    ext_a,
    ext_b,
    gext,
    land_row,
    land_col,
    land_corner,
    probe_rolled,
    first_cut,
    wave_mid,
    wave_back,
    pieces,
    probe_acc,
    land_pair,
    land_plane,
    land_line,
    shard,
    probe_sum,
    in_send,
    in_recv,
    own_sem,
    out_send,
    out_recv,
    write_sem,
    pair_sem,
    plane_send,
    plane_recv,
    line_send,
    line_recv,
    back_send,
    back_recv,
):
    g, m = lax.axis_index("group"), lax.axis_index("member")
    left, right = (g, lax.rem(m + nm - 1, nm)), (g, lax.rem(m + 1, nm))
    up, down = (lax.rem(g + ng - 1, ng), m), (lax.rem(g + 1, ng), m)
    core, chip = lax.rem(m, 2), m // 2
    chips = nm // 2
    blocks = tile // size
    modes = probe_ref.shape[0] // 2
    ext = (ext_a, ext_b)

    def remote(src, dst, send, recv, device):
        return pltpu.make_async_remote_copy(
            src_ref=src, dst_ref=dst, send_sem=send, recv_sem=recv, device_id=device, device_id_type=MESH
        )

    barrier = pltpu.get_barrier_semaphore()
    low, wide, edge = pl.ds(tile, size), pl.ds(0, tile), pl.ds(0, size)
    rest = pl.ds(size, tile - size)
    own_copies = [
        [
            pltpu.make_async_copy(object_ref.at[s, :, :, pl.ds(j * size, size)], ext[s].at[j, :, wide], own_sem.at[s, j])
            for j in range(blocks)
        ]
        for s in range(2)
    ]
    for copy in own_copies[0] + own_copies[1]:
        copy.start()
    greeted = [left, right]
    greeted += [(g, 2 * lax.rem(chip + d, chips) + core) for d in range(1, chips)]
    greeted += [(lax.rem(g + d, ng), m) for d in range(1, ng)]
    for device in greeted:
        pl.semaphore_signal(barrier, inc=1, device_id=device, device_id_type=MESH)
    pl.semaphore_wait(barrier, len(greeted))

    rims = []
    for s in range(2):
        rims.append(
            [
                remote(object_ref.at[s, :, edge, pl.ds(j * size, size)], ext[s].at[j, :, low], in_send.at[s, j], in_recv.at[s, j], up)
                for j in range(blocks)
            ]
            + [
                remote(object_ref.at[s, :, :, edge], ext[s].at[blocks, :, wide], in_send.at[s, blocks], in_recv.at[s, blocks], left),
                remote(ext[s].at[0, :, low], ext[s].at[blocks, :, low], in_send.at[s, blocks + 1], in_recv.at[s, blocks + 1], left),
            ]
        )
        for copy in rims[s][: blocks + 1]:
            copy.start()

    def place(p):
        row, col = offset_ref[p, 0], offset_ref[p, 1]
        return row, col // size, lax.rem(col, size)

    def roll_probe(p, carry):
        _, _, cs = place(p)
        for plane in range(2 * modes):
            probe_rolled[p, plane] = pltpu.roll(probe_ref[plane], cs, axis=1)
        return carry

    lax.fori_loop(0, cap, roll_probe, 0)

    def from_start(cs):
        return lax.broadcasted_iota(jnp.int32, (size, size), 1) >= cs

    def cut(p, s):
        row, bj, cs = place(p)
        inside = from_start(cs)
        rows = pl.ds(row, size)
        return tuple(jnp.where(inside, ext[s][bj, plane, rows], ext[s][bj + 1, plane, rows]) for plane in range(2))

    def waves_of(ref, p):
        return [(ref[p, 2 * k], ref[p, 2 * k + 1]) for k in range(modes)]

    def store_waves(ref, p, waves):
        for k in range(modes):
            ref[p, 2 * k] = waves[k][0]
            ref[p, 2 * k + 1] = waves[k][1]

    def store_pieces(p, grad):
        _, _, cs = place(p)
        inside = from_start(cs)
        for plane in range(2):
            pieces[p, 0, plane, pl.ds(size, size)] = jnp.where(inside, grad[plane], 0.0)
            pieces[p, 1, plane, pl.ds(size, size)] = jnp.where(inside, 0.0, grad[plane])

    def clear_pieces(p, carry):
        for n in (0, 2):
            pieces[p, :, :, pl.ds(n * size, size)] = jnp.zeros((2, 2, size, size), F32)
        return carry

    lax.fori_loop(0, cap, clear_pieces, 0)

    def assemble(s, i, j):
        total = None
        for p in range(cap):
            row, bj, _ = place(p)
            b = j - bj
            inside = (b >= 0) & (b <= 1)
            start = jnp.where(inside, jnp.clip((i + 1) * size - row, 0, 2 * size), 0)
            part = pieces[p, jnp.where(inside, b, 0), :, pl.ds(start, size)]
            total = part if total is None else total + part
        gext[
            s, :, pl.ds(pl.multiple_of(i * size, size), size), pl.ds(pl.multiple_of(j * size, size), size)
        ] = total

    def assemble_many(s, n, where):
        def one(t, carry):
            assemble(s, *where(t))
            return carry

        lax.fori_loop(0, n, one, 0)

    fourier, fourier_conj, spread, spread_conj = (0, 1), (1, 0), (2, 3), (3, 2)

    def arrive(s):
        rims[s][0].wait_recv()
        rims[s][blocks + 1].start()
        for copy in own_copies[s]:
            copy.wait()
        for copy in rims[s][1:]:
            copy.wait_recv()

    arrive(0)

    def stage_one(t, carry):
        waves = []
        for q in range(PAIR):
            p = t * PAIR + q
            patch = cut(p, 0)
            first_cut[p, 0], first_cut[p, 1] = patch
            waves += [times(w, patch) for w in waves_of(probe_rolled, p)]
        waves = two_sided(tables, *spread, waves)
        for q in range(PAIR):
            store_waves(wave_mid, t * PAIR + q, waves[q * modes : (q + 1) * modes])
        return carry

    lax.fori_loop(0, cap // PAIR, stage_one, 0)

    arrive(1)

    own_count = count_ref[g, m]

    def stage_two(t, carry):
        patches, mids, waves = [], [], []
        for q in range(PAIR):
            p = t * PAIR + q
            patches.append(cut(p, 1))
            mids.append(waves_of(wave_mid, p))
            waves += [times(w, patches[q]) for w in mids[q]]
        far = two_sided(tables, *fourier, waves)
        waves = []
        for q in range(PAIR):
            p = t * PAIR + q
            intensity = None
            for w in far[q * modes : (q + 1) * modes]:
                power = w[0] * w[0] + w[1] * w[1]
                intensity = power if intensity is None else intensity + power
            valid = jnp.where(p < own_count, 2.0, 0.0).astype(F32)
            slope = valid * (1.0 - measured_ref[p] * lax.rsqrt(intensity + 1.0))
            waves += [(w[0] * slope, w[1] * slope) for w in far[q * modes : (q + 1) * modes]]
        back = two_sided(tables, *fourier_conj, waves)
        for q in range(PAIR):
            p = t * PAIR + q
            own = back[q * modes : (q + 1) * modes]
            grad = None
            for mid, w in zip(mids[q], own):
                term = conj_times(mid, w)
                grad = term if grad is None else plus(grad, term)
            store_pieces(p, grad)
            store_waves(wave_back, p, [conj_times(patches[q], w) for w in own])
        return carry

    lax.fori_loop(0, cap // PAIR, stage_two, 0)

    homes = []
    for s in range(2):
        homes.append(
            (
                remote(gext.at[s, :, low, rest], land_row.at[s, :, :, rest], out_send.at[s, 0], out_recv.at[s, 0], down),
                remote(gext.at[s, :, low, low], land_corner.at[s], out_send.at[s, 1], out_recv.at[s, 1], right),
                remote(gext.at[s, :, wide, low], land_col.at[s], out_send.at[s, 2], out_recv.at[s, 2], right),
                remote(gext.at[s, :, low, edge], land_row.at[s, :, :, edge], out_send.at[s, 3], out_recv.at[s, 3], down),
            )
        )

    def send_rims(s):
        assemble_many(s, blocks, lambda t: (blocks, t + 1))
        homes[s][1].start()
        homes[s][0].start()
        assemble_many(s, blocks, lambda t: (t, blocks))
        homes[s][2].start()
        assemble(s, blocks, 0)

    def send_corner(s):
        homes[s][1].wait_recv()
        gext[s, :, low, edge] += land_corner[s]
        homes[s][3].start()

    send_rims(1)
    send_corner(1)
    assemble_many(1, blocks * blocks, lambda t: (t // blocks, lax.rem(t, blocks)))

    probe_acc[...] = jnp.zeros(probe_acc.shape, F32)

    def stage_three(t, carry):
        waves = []
        for q in range(PAIR):
            waves += waves_of(wave_back, t * PAIR + q)
        waves = two_sided(tables, *spread_conj, waves)
        turned_back = [[] for _ in range(PAIR * modes)]
        for q in range(PAIR):
            p = t * PAIR + q
            patch = (first_cut[p, 0], first_cut[p, 1])
            grad = None
            for k, (probe, w) in enumerate(zip(waves_of(probe_rolled, p), waves[q * modes : (q + 1) * modes])):
                term = conj_times(probe, w)
                grad = term if grad is None else plus(grad, term)
                turned = turned_back[q * modes + k]
                for plane, x in enumerate(conj_times(patch, w)):
                    turned.append(x)
            store_pieces(p, grad)
        for k in range(modes):
            for plane in range(2):
                total = None
                for q in range(PAIR):
                    _, _, cs = place(t * PAIR + q)
                    x = pltpu.roll(turned_back[q * modes + k][plane], lax.rem(size - cs, size), axis=1)
                    total = x if total is None else total + x
                probe_acc[pl.ds((2 * k + plane) * size, size), :] += total
        return carry

    lax.fori_loop(0, cap // PAIR, stage_three, 0)
    send_rims(0)

    rows = probe_acc.shape[0]
    half, step = rows // 2, rows // 2 // chips
    partner = (g, m + 1 - 2 * core)
    pair = remote(
        probe_acc.at[pl.ds(pl.multiple_of((1 - core) * half, half), half)], land_pair, pair_sem.at[0], pair_sem.at[1], partner
    )
    pair.start()
    send_corner(0)
    pair.wait_recv()
    mine = pl.ds(pl.multiple_of(core * half, half), half)
    land_pair[...] += probe_acc[mine]
    to_plane, to_line, to_back = [], [], []
    for d in range(1, chips):
        other = lax.rem(chip + d, chips)
        to_plane.append(
            remote(
                land_pair.at[pl.ds(pl.multiple_of(other * step, step), step)],
                land_plane.at[chip],
                plane_send.at[d],
                plane_recv.at[d],
                (g, 2 * other + core),
            )
        )
        to_plane[-1].start()
    land_plane[chip] = land_pair[pl.ds(pl.multiple_of(chip * step, step), step)]
    assemble_many(0, blocks * blocks, lambda t: (t // blocks, lax.rem(t, blocks)))
    for copy in to_plane:
        copy.wait_recv()
    total = land_plane[0]
    for n in range(1, chips):
        total = total + land_plane[n]
    shard[...] = total
    land_line[g] = total
    for d in range(1, ng):
        to_line.append(
            remote(shard, land_line.at[g], line_send.at[d], line_recv.at[d], (lax.rem(g + d, ng), m))
        )
        to_line[-1].start()
    positions = jnp.sum(counts_ref[...].astype(F32), keepdims=True)
    for copy in to_line:
        copy.wait_recv()
    total = land_line[0]
    for n in range(1, ng):
        total = total + land_line[n]
    spot = pl.ds(pl.multiple_of(core * half + chip * step, step), step)
    probe_sum[spot] = total / jnp.sqrt(positions)
    for d in range(1, chips):
        other = lax.rem(chip + d, chips)
        to_back.append(
            remote(probe_sum.at[spot], probe_sum.at[spot], back_send.at[d], back_recv.at[d], (g, 2 * other + core))
        )
        to_back[-1].start()

    writes = []

    def finish(s):
        for n in (0, 2, 3):
            homes[s][n].wait_recv()
        gext[s, :, pl.ds(0, size), wide] += land_row[s]
        gext[s, :, wide, pl.ds(0, size)] += land_col[s]
        writes.append(pltpu.make_async_copy(gext.at[s, :, wide, wide], grad_ref.at[s], write_sem.at[s]))
        writes[-1].start()

    finish(1)
    for copy in to_back:
        copy.wait_recv()
    share = remote(probe_sum.at[mine], probe_sum.at[mine], pair_sem.at[2], pair_sem.at[3], partner)
    share.start()
    finish(0)
    share.wait_recv()
    for plane in range(2 * modes):
        probe_grad_ref[plane] = probe_sum[pl.ds(plane * size, size), :]

    for s in range(2):
        for copy in [*rims[s], *homes[s]]:
            copy.wait_send()
    for copy in to_plane + to_line + to_back + [pair, share]:
        copy.wait_send()
    for copy in writes:
        copy.wait()


def per_device(object_tiles, probe_modes, measured, slot_offset, slot_count):
    ng, nm = lax.axis_size("group"), lax.axis_size("member")
    tile = object_tiles.shape[-1]
    size = probe_modes.shape[-1]
    cap = measured.shape[2]
    planes = 2 * probe_modes.shape[0]
    ext = tile + size
    blocks = tile // size
    chips = nm // 2
    rows = planes * size
    step = rows // 2 // chips
    tables = jnp.asarray(make_tables(size))
    vmem, smem = pl.BlockSpec(memory_space=pltpu.VMEM), pl.BlockSpec(memory_space=pltpu.SMEM)
    hbm = pl.BlockSpec(memory_space=pl.ANY)
    dma = pltpu.SemaphoreType.DMA

    def body(*refs):
        kernel(ng, nm, tile, size, cap, *refs)

    grad, probe_grad = pl.pallas_call(
        body,
        out_shape=(
            jax.ShapeDtypeStruct(object_tiles.shape, F32),
            jax.ShapeDtypeStruct((planes, size, size), F32),
        ),
        in_specs=[smem, smem, vmem, hbm, vmem, vmem, vmem],
        out_specs=(hbm, vmem),
        scratch_shapes=[
            pltpu.VMEM((blocks + 1, 2, ext, size), F32),
            pltpu.VMEM((blocks + 1, 2, ext, size), F32),
            pltpu.VMEM((2, 2, ext, ext), F32),
            pltpu.VMEM((2, 2, size, tile), F32),
            pltpu.VMEM((2, 2, tile, size), F32),
            pltpu.VMEM((2, 2, size, size), F32),
            pltpu.VMEM((cap, planes, size, size), F32),
            pltpu.VMEM((cap, 2, size, size), F32),
            pltpu.VMEM((cap, planes, size, size), F32),
            pltpu.VMEM((cap, planes, size, size), F32),
            pltpu.VMEM((cap, 2, 2, 3 * size, size), F32),
            pltpu.VMEM((rows, size), F32),
            pltpu.VMEM((rows // 2, size), F32),
            pltpu.VMEM((chips, step, size), F32),
            pltpu.VMEM((ng, step, size), F32),
            pltpu.VMEM((step, size), F32),
            pltpu.VMEM((rows, size), F32),
            dma((2, blocks + 2)),
            dma((2, blocks + 2)),
            dma((2, blocks)),
            dma((2, 4)),
            dma((2, 4)),
            dma((2,)),
            dma((4,)),
            dma((chips,)),
            dma((chips,)),
            dma((ng,)),
            dma((ng,)),
            dma((chips,)),
            dma((chips,)),
        ],
        compiler_params=pltpu.CompilerParams(
            collective_id=0, has_side_effects=True, vmem_limit_bytes=48 * 1024 * 1024
        ),
    )(
        slot_offset.reshape(cap, 2),
        slot_count,
        slot_count,
        object_tiles,
        probe_modes.reshape(planes, size, size),
        measured.reshape(cap, size, size),
        tables,
    )
    return grad, probe_grad.reshape(probe_modes.shape)


def solution(mesh):
    placed = (
        P(None, None, "group", "member"),
        P(),
        P("group", "member", None, None, None),
        P("group", "member", None, None),
        P(),
    )
    return jax.shard_map(
        per_device,
        mesh=mesh,
        in_specs=placed,
        out_specs=(P(None, None, "group", "member"), P()),
        check_vma=False,
    )
```

time: 699 us -> 87.6 us (0.13)
  waiting for transfers between devices: 359 us -> 0 us
  matrix products: 183 us -> 0 us
  Pallas kernels: 0 us -> 76.7 us
  local copies, waits for them, and re-layouts: 65.6 us -> 10 us
  loops' own time: 33.7 us -> 0 us
  other arithmetic: 29.5 us -> 0 us
  between operations: 14.9 us -> 0.64 us
  starting transfers between devices: 9.9 us -> 0 us
    psum x1 -> x0, waiting for transfers between devices: 308 us -> none  [per_device(): probe_total = lax.psum(probe_acc, ('group', 'member'))]
    dot_general x336 -> x0, matrix products: 183 us -> none  [the longest x168 92.9 us: from_left(): return jnp.einsum('ij,bjk->bik', matrix, batch, precision=highest)]
    pallas_call x0 -> x1, Pallas kernels: none -> 76.7 us  [per_device(): pl.pallas_call(body, out_shape=(jax.ShapeDtypeStruct(object_tiles.shape,...]
    ppermute x4 -> x0, waiting for transfers between devices: 50.3 us -> none  [from_behind(): return lax.ppermute(block, axis, route)]
    another operation x1 -> x0, loops' own time: 33.7 us -> none  [per_device(): lax.fori_loop(0, own_count, own_step, (grad_start, probe_start))]
    dynamic_update_slice x7 -> x0, local copies, waits for them, and re-layouts: 30.1 us -> none  [add_patch(): return lax.dynamic_update_slice(grad_ext, current + update, starts)]
    mul x21 -> x0, local copies, waits for them, and re-layouts: 10.1 us -> none  [the longest x7 8.79 us: position_loss(): next_imag = wave_real * obj_imag + wave_imag * obj_real]
    ppermute x4 -> x0, starting transfers between devices: 9.87 us -> none  [from_behind(): return lax.ppermute(block, axis, route)]
  transfers between devices with their start and end apart: 5 -> 0, of which waited for: 4 -> 0; matrix products, arithmetic and copies ran while one was open for 1% -> 0% of each run, Pallas kernels for 0% -> 0%
where the time goes in v1:
time: 87.6 us; the launch traced here: 87.4 us
  Pallas kernels  76.7 us (88%)
  local copies, waits for them, and re-layouts  10 us (11%)
    pallas_call x1, Pallas kernels, per_device(): pl.pallas_call(body, out_shape=(jax.ShapeDtypeStruct(object_tiles.shape,...  76.7 us
    unnamed x10, local copies, waits for them, and re-layouts  9.24 us

profile of v1, /device:TPU:1, one launch (start us, length us, event | category | flops | bytes accessed | tf_op | source)
XLA Modules:
  0.0 87.4 jit_solution(2951931592839422993)
XLA Ops:
  0.6 0.8 copy.8.refs_0_
  1.4 0.0 copy-start
  1.4 1.2 %copy-done = bf16[4,2,256,256]{3,2,1,0:T(8,128)(2,1)S(1)} copy-done((bf16[4,2,256,256]{3,2,1,0:T(8,128)(2,1)S(1)}, bf16[4,2,256,256]{3,2,1,0:T(8,128)(2,1)}, u32[]{:S(2)}) %copy-start) | copy-done | bytes 1048600
  2.6 0.0 copy-start.1
  2.6 1.0 %copy-done.1 = f32[1,1,8,128,128]{4,3,2,1,0:T(8,128)S(1)} copy-done((f32[1,1,8,128,128]{4,3,2,1,0:T(8,128)S(1)}, f32[1,1,8,128,128]{4,3,2,1,0:T(8,128)}, u32[]{:S(2)}) %copy-start.1) | copy-done | bytes 524312
  3.7 0.0 copy-start.2
  3.7 0.9 %copy-done.2 = f32[2,2,128,128]{3,2,1,0:T(8,128)S(1)} copy-done((f32[2,2,128,128]{3,2,1,0:T(8,128)S(1)}, f32[2,2,128,128]{3,2,1,0:T(8,128)}, u32[]{:S(2)}) %copy-start.2) | copy-done | bytes 262168
  4.6 0.0 copy-start.3
  4.6 0.7 copy-done.3
  5.3 76.7 %shard_map.77 = (f32[2,2,512,512]{3,2,1,0:T(8,128)}, f32[4,128,128]{2,1,0:T(8,128)S(1)}) custom-call(s32[8,2]{1,0:T(8,128)S(1)} %copy.8.refs_0_, s32[8,32]{1,0:T(8,128)S(1)} %copy-done.3, s32[8,32]{1,0:T(8,128)S(1)} %copy-done.3, f32[2,2,512,512]{3,2,1,0:T(8,128)} %refs_3_.1, f32[4,128,128]{2,1,0:T(8,128)S(1)} %bitcast.5, f32[8,128,128]{2,1,0:T(8,128)S(1)} %bitcast.4, ...), custom_call_target="tpu_custom_call" | custom-call | tf_op jit(solution)/shard_map/pallas_call | solution.py:456
  82.0 4.6 %copy.11 = f32[2,2,512,512]{3,2,1,0:T(8,128)} copy(f32[2,2,512,512]{3,2,1,0:T(8,128)} %get-tuple-element.8) | data formatting | bytes 8388608
  86.7 0.7 copy.12
Async XLA Ops:
  1.4 1.2 %copy-start = (bf16[4,2,256,256]{3,2,1,0:T(8,128)(2,1)S(1)}, bf16[4,2,256,256]{3,2,1,0:T(8,128)(2,1)}, u32[]{:S(2)}) copy-start(bf16[4,2,256,256]{3,2,1,0:T(8,128)(2,1)} %constant.2.clone.refs_6_) | copy-start | bytes 3145732
  2.6 1.0 %copy-start.1 = (f32[1,1,8,128,128]{4,3,2,1,0:T(8,128)S(1)}, f32[1,1,8,128,128]{4,3,2,1,0:T(8,128)}, u32[]{:S(2)}) copy-start(f32[1,1,8,128,128]{4,3,2,1,0:T(8,128)} %param.8) | copy-start | bytes 1572868
  3.7 0.9 %copy-start.2 = (f32[2,2,128,128]{3,2,1,0:T(8,128)S(1)}, f32[2,2,128,128]{3,2,1,0:T(8,128)}, u32[]{:S(2)}) copy-start(f32[2,2,128,128]{3,2,1,0:T(8,128)} %param.7) | copy-start | bytes 786436
  4.6 0.7 copy-start.3

commit v2 on v1

--- a/solution.py
+++ b/solution.py
@@ -13,7 +13,7 @@
 F32 = jnp.float32
 BF16 = jnp.bfloat16
 FRESNEL_RATE = 0.5
-PAIR = 2
+PAIR = 4
 
 
 def make_tables(size):
@@ -79,18 +79,25 @@
     tile,
     size,
     cap,
+    offset_hbm,
+    counts_hbm,
+    object_ref,
+    probe_hbm,
+    measured_hbm,
+    tables_hbm,
+    grad_ref,
+    probe_grad_ref,
     offset_ref,
     count_ref,
     counts_ref,
-    object_ref,
     probe_ref,
     measured_ref,
     tables,
-    grad_ref,
-    probe_grad_ref,
+    load_sem,
     ext_a,
     ext_b,
-    gext,
+    rim_row,
+    rim_col,
     land_row,
     land_col,
     land_corner,
@@ -102,20 +109,19 @@
     probe_acc,
     land_pair,
     land_plane,
-    land_line,
-    shard,
+    part_sum,
+    land_z,
     probe_sum,
     in_send,
     in_recv,
     own_sem,
     out_send,
     out_recv,
-    write_sem,
     pair_sem,
     plane_send,
     plane_recv,
-    line_send,
-    line_recv,
+    z_send,
+    z_recv,
     back_send,
     back_recv,
 ):
@@ -124,9 +130,13 @@
     up, down = (lax.rem(g + ng - 1, ng), m), (lax.rem(g + 1, ng), m)
     core, chip = lax.rem(m, 2), m // 2
     chips = nm // 2
+    partner = (g, m + 1 - 2 * core)
     blocks = tile // size
     modes = probe_ref.shape[0] // 2
     ext = (ext_a, ext_b)
+
+    def spot_of(start, length):
+        return pl.ds(pl.multiple_of(start, 8), length)
 
     def remote(src, dst, send, recv, device):
         return pltpu.make_async_remote_copy(
@@ -143,13 +153,26 @@
         ]
         for s in range(2)
     ]
-    for copy in own_copies[0] + own_copies[1]:
-        copy.start()
-    greeted = [left, right]
+    greeted = [up, down, left, right]
     greeted += [(g, 2 * lax.rem(chip + d, chips) + core) for d in range(1, chips)]
-    greeted += [(lax.rem(g + d, ng), m) for d in range(1, ng)]
+    greeted += [(lax.rem(g + d, ng), m) for d in range(2, ng - 1)]
     for device in greeted:
         pl.semaphore_signal(barrier, inc=1, device_id=device, device_id_type=MESH)
+    loads = [
+        pltpu.make_async_copy(src, dst, load_sem.at[n])
+        for n, (src, dst) in enumerate(
+            (
+                (offset_hbm, offset_ref),
+                (probe_hbm, probe_ref),
+                (tables_hbm, tables),
+                (measured_hbm, measured_ref),
+                (counts_hbm, count_ref),
+                (counts_hbm, counts_ref),
+            )
+        )
+    ]
+    for copy in loads + own_copies[0] + own_copies[1]:
+        copy.start()
     pl.semaphore_wait(barrier, len(greeted))
 
     rims = []
@@ -168,8 +191,11 @@
             copy.start()
 
     def place(p):
-        row, col = offset_ref[p, 0], offset_ref[p, 1]
+        row, col = offset_ref[0, 0, 0, p], offset_ref[0, 0, 1, p]
         return row, col // size, lax.rem(col, size)
+
+    for copy in loads:
+        copy.wait()
 
     def roll_probe(p, carry):
         _, _, cs = place(p)
@@ -196,16 +222,17 @@
             ref[p, 2 * k] = waves[k][0]
             ref[p, 2 * k + 1] = waves[k][1]
 
-    def store_pieces(p, grad):
+    def store_pieces(s, p, grad):
         _, _, cs = place(p)
         inside = from_start(cs)
         for plane in range(2):
-            pieces[p, 0, plane, pl.ds(size, size)] = jnp.where(inside, grad[plane], 0.0)
-            pieces[p, 1, plane, pl.ds(size, size)] = jnp.where(inside, 0.0, grad[plane])
+            pieces[s, p, 0, plane, pl.ds(size, size)] = jnp.where(inside, grad[plane], 0.0)
+            pieces[s, p, 1, plane, pl.ds(size, size)] = jnp.where(inside, 0.0, grad[plane])
 
     def clear_pieces(p, carry):
         for n in (0, 2):
-            pieces[p, :, :, pl.ds(n * size, size)] = jnp.zeros((2, 2, size, size), F32)
+            for s in range(2):
+                pieces[s, p, :, :, pl.ds(n * size, size)] = jnp.zeros((2, 2, size, size), F32)
         return carry
 
     lax.fori_loop(0, cap, clear_pieces, 0)
@@ -217,18 +244,29 @@
             b = j - bj
             inside = (b >= 0) & (b <= 1)
             start = jnp.where(inside, jnp.clip((i + 1) * size - row, 0, 2 * size), 0)
-            part = pieces[p, jnp.where(inside, b, 0), :, pl.ds(start, size)]
+            part = pieces[s, p, jnp.where(inside, b, 0), :, pl.ds(start, size)]
             total = part if total is None else total + part
-        gext[
-            s, :, pl.ds(pl.multiple_of(i * size, size), size), pl.ds(pl.multiple_of(j * size, size), size)
-        ] = total
-
-    def assemble_many(s, n, where):
-        def one(t, carry):
-            assemble(s, *where(t))
+        return total
+
+    def span(t):
+        return pl.ds(pl.multiple_of(t * size, size), size)
+
+    def assemble_low(s, j):
+        rim_row[s, :, :, span(j)] = assemble(s, blocks, j)
+
+    def assemble_wide(s, i):
+        rim_col[s, :, span(i)] = assemble(s, i, blocks)
+
+    def assemble_own(s, t):
+        i, j = t // blocks, lax.rem(t, blocks)
+        grad_ref[s, :, span(i), span(j)] = assemble(s, i, j)
+
+    def assemble_many(s, n, one):
+        def step(t, carry):
+            one(s, t)
             return carry
 
-        lax.fori_loop(0, n, one, 0)
+        lax.fori_loop(0, n, step, 0)
 
     fourier, fourier_conj, spread, spread_conj = (0, 1), (1, 0), (2, 3), (3, 2)
 
@@ -286,7 +324,7 @@
             for mid, w in zip(mids[q], own):
                 term = conj_times(mid, w)
                 grad = term if grad is None else plus(grad, term)
-            store_pieces(p, grad)
+            store_pieces(1, p, grad)
             store_waves(wave_back, p, [conj_times(patches[q], w) for w in own])
         return carry
 
@@ -296,29 +334,25 @@
     for s in range(2):
         homes.append(
             (
-                remote(gext.at[s, :, low, rest], land_row.at[s, :, :, rest], out_send.at[s, 0], out_recv.at[s, 0], down),
-                remote(gext.at[s, :, low, low], land_corner.at[s], out_send.at[s, 1], out_recv.at[s, 1], right),
-                remote(gext.at[s, :, wide, low], land_col.at[s], out_send.at[s, 2], out_recv.at[s, 2], right),
-                remote(gext.at[s, :, low, edge], land_row.at[s, :, :, edge], out_send.at[s, 3], out_recv.at[s, 3], down),
+                remote(rim_row.at[s, :, :, rest], land_row.at[s, :, :, rest], out_send.at[s, 0], out_recv.at[s, 0], down),
+                remote(rim_row.at[s, :, :, low], land_corner.at[s], out_send.at[s, 1], out_recv.at[s, 1], right),
+                remote(rim_col.at[s], land_col.at[s], out_send.at[s, 2], out_recv.at[s, 2], right),
+                remote(rim_row.at[s, :, :, edge], land_row.at[s, :, :, edge], out_send.at[s, 3], out_recv.at[s, 3], down),
             )
         )
 
-    def send_rims(s):
-        assemble_many(s, blocks, lambda t: (blocks, t + 1))
-        homes[s][1].start()
-        homes[s][0].start()
-        assemble_many(s, blocks, lambda t: (t, blocks))
-        homes[s][2].start()
-        assemble(s, blocks, 0)
-
     def send_corner(s):
         homes[s][1].wait_recv()
-        gext[s, :, low, edge] += land_corner[s]
+        rim_row[s, :, :, edge] += land_corner[s]
         homes[s][3].start()
 
-    send_rims(1)
-    send_corner(1)
-    assemble_many(1, blocks * blocks, lambda t: (t // blocks, lax.rem(t, blocks)))
+    assemble_many(1, blocks - 1, lambda s, t: assemble_low(s, t + 1))
+    homes[1][0].start()
+    assemble_low(1, blocks)
+    homes[1][1].start()
+    assemble_low(1, 0)
+    assemble_many(1, blocks, assemble_wide)
+    homes[1][2].start()
 
     probe_acc[...] = jnp.zeros(probe_acc.shape, F32)
 
@@ -338,7 +372,7 @@
                 turned = turned_back[q * modes + k]
                 for plane, x in enumerate(conj_times(patch, w)):
                     turned.append(x)
-            store_pieces(p, grad)
+            store_pieces(0, p, grad)
         for k in range(modes):
             for plane in range(2):
                 total = None
@@ -350,74 +384,69 @@
         return carry
 
     lax.fori_loop(0, cap // PAIR, stage_three, 0)
-    send_rims(0)
 
     rows = probe_acc.shape[0]
-    half, step = rows // 2, rows // 2 // chips
-    partner = (g, m + 1 - 2 * core)
-    pair = remote(
-        probe_acc.at[pl.ds(pl.multiple_of((1 - core) * half, half), half)], land_pair, pair_sem.at[0], pair_sem.at[1], partner
-    )
+    half = rows // 2
+    pair = remote(probe_acc.at[spot_of((1 - core) * half, half)], land_pair, pair_sem.at[0], pair_sem.at[1], partner)
     pair.start()
-    send_corner(0)
+    assemble_many(0, blocks + 1, assemble_low)
+    homes[0][1].start()
+    send_corner(1)
     pair.wait_recv()
-    mine = pl.ds(pl.multiple_of(core * half, half), half)
-    land_pair[...] += probe_acc[mine]
-    to_plane, to_line, to_back = [], [], []
+    land_pair[...] += probe_acc[spot_of(core * half, half)]
+
+    sent = [pair]
+
+    def added(land, n, copies):
+        for copy in copies:
+            copy.wait_recv()
+        sent.extend(copies)
+        total = land[0]
+        for t in range(1, n):
+            total = total + land[t]
+        return total
+
+    part = half // chips
+    copies = []
     for d in range(1, chips):
         other = lax.rem(chip + d, chips)
-        to_plane.append(
-            remote(
-                land_pair.at[pl.ds(pl.multiple_of(other * step, step), step)],
-                land_plane.at[chip],
-                plane_send.at[d],
-                plane_recv.at[d],
-                (g, 2 * other + core),
-            )
-        )
-        to_plane[-1].start()
-    land_plane[chip] = land_pair[pl.ds(pl.multiple_of(chip * step, step), step)]
-    assemble_many(0, blocks * blocks, lambda t: (t // blocks, lax.rem(t, blocks)))
-    for copy in to_plane:
-        copy.wait_recv()
-    total = land_plane[0]
-    for n in range(1, chips):
-        total = total + land_plane[n]
-    shard[...] = total
-    land_line[g] = total
+        to = (g, 2 * other + core)
+        copies.append(remote(land_pair.at[spot_of(other * part, part)], land_plane.at[chip], plane_send.at[d], plane_recv.at[d], to))
+        copies[-1].start()
+    land_plane[chip] = land_pair[spot_of(chip * part, part)]
+    assemble_many(0, blocks, assemble_wide)
+    homes[0][2].start()
+    part_sum[...] = added(land_plane, chips, copies)
+    land_z[g] = part_sum[...]
+    copies = []
     for d in range(1, ng):
-        to_line.append(
-            remote(shard, land_line.at[g], line_send.at[d], line_recv.at[d], (lax.rem(g + d, ng), m))
-        )
-        to_line[-1].start()
+        to = (lax.rem(g + d, ng), m)
+        copies.append(remote(part_sum, land_z.at[g], z_send.at[d], z_recv.at[d], to))
+        copies[-1].start()
+    homes[0][0].start()
+    send_corner(0)
+    assemble_many(1, blocks * blocks, assemble_own)
+    assemble_many(0, blocks * blocks, assemble_own)
     positions = jnp.sum(counts_ref[...].astype(F32), keepdims=True)
-    for copy in to_line:
-        copy.wait_recv()
-    total = land_line[0]
-    for n in range(1, ng):
-        total = total + land_line[n]
-    spot = pl.ds(pl.multiple_of(core * half + chip * step, step), step)
-    probe_sum[spot] = total / jnp.sqrt(positions)
+    spot = spot_of(core * half + chip * part, part)
+    probe_sum[spot] = added(land_z, ng, copies) / jnp.sqrt(positions)
+    copies = []
     for d in range(1, chips):
-        other = lax.rem(chip + d, chips)
-        to_back.append(
-            remote(probe_sum.at[spot], probe_sum.at[spot], back_send.at[d], back_recv.at[d], (g, 2 * other + core))
-        )
-        to_back[-1].start()
-
-    writes = []
+        to = (g, 2 * lax.rem(chip + d, chips) + core)
+        copies.append(remote(probe_sum.at[spot], probe_sum.at[spot], back_send.at[d], back_recv.at[d], to))
+        copies[-1].start()
 
     def finish(s):
         for n in (0, 2, 3):
             homes[s][n].wait_recv()
-        gext[s, :, pl.ds(0, size), wide] += land_row[s]
-        gext[s, :, wide, pl.ds(0, size)] += land_col[s]
-        writes.append(pltpu.make_async_copy(gext.at[s, :, wide, wide], grad_ref.at[s], write_sem.at[s]))
-        writes[-1].start()
+        grad_ref[s, :, pl.ds(0, size), wide] += land_row[s]
+        grad_ref[s, :, wide, pl.ds(0, size)] += land_col[s]
 
     finish(1)
-    for copy in to_back:
+    for copy in copies:
         copy.wait_recv()
+    sent.extend(copies)
+    mine = spot_of(core * half, half)
     share = remote(probe_sum.at[mine], probe_sum.at[mine], pair_sem.at[2], pair_sem.at[3], partner)
     share.start()
     finish(0)
@@ -428,10 +457,8 @@
     for s in range(2):
         for copy in [*rims[s], *homes[s]]:
             copy.wait_send()
-    for copy in to_plane + to_line + to_back + [pair, share]:
+    for copy in [*sent, share]:
         copy.wait_send()
-    for copy in writes:
-        copy.wait()
 
 
 def per_device(object_tiles, probe_modes, measured, slot_offset, slot_count):
@@ -446,8 +473,8 @@
     rows = planes * size
     step = rows // 2 // chips
     tables = jnp.asarray(make_tables(size))
-    vmem, smem = pl.BlockSpec(memory_space=pltpu.VMEM), pl.BlockSpec(memory_space=pltpu.SMEM)
-    hbm = pl.BlockSpec(memory_space=pl.ANY)
+    vmem = pl.BlockSpec(memory_space=pltpu.VMEM)
+    hbm = pl.BlockSpec(memory_space=pltpu.HBM)
     dma = pltpu.SemaphoreType.DMA
 
     def body(*refs):
@@ -456,15 +483,23 @@
     grad, probe_grad = pl.pallas_call(
         body,
         out_shape=(
-            jax.ShapeDtypeStruct(object_tiles.shape, F32),
-            jax.ShapeDtypeStruct((planes, size, size), F32),
+            pltpu.VMEM(object_tiles.shape, F32),
+            pltpu.VMEM((planes, size, size), F32),
         ),
-        in_specs=[smem, smem, vmem, hbm, vmem, vmem, vmem],
-        out_specs=(hbm, vmem),
+        in_specs=[hbm] * 6,
+        out_specs=(vmem, vmem),
         scratch_shapes=[
+            pltpu.SMEM((1, 1, 2, cap), jnp.int32),
+            pltpu.SMEM(slot_count.shape, jnp.int32),
+            pltpu.VMEM(slot_count.shape, jnp.int32),
+            pltpu.VMEM((planes, size, size), F32),
+            pltpu.VMEM((cap, size, size), F32),
+            pltpu.VMEM(tables.shape, BF16),
+            dma((6,)),
             pltpu.VMEM((blocks + 1, 2, ext, size), F32),
             pltpu.VMEM((blocks + 1, 2, ext, size), F32),
-            pltpu.VMEM((2, 2, ext, ext), F32),
+            pltpu.VMEM((2, 2, size, ext), F32),
+            pltpu.VMEM((2, 2, tile, size), F32),
             pltpu.VMEM((2, 2, size, tile), F32),
             pltpu.VMEM((2, 2, tile, size), F32),
             pltpu.VMEM((2, 2, size, size), F32),
@@ -472,19 +507,18 @@
             pltpu.VMEM((cap, 2, size, size), F32),
             pltpu.VMEM((cap, planes, size, size), F32),
             pltpu.VMEM((cap, planes, size, size), F32),
-            pltpu.VMEM((cap, 2, 2, 3 * size, size), F32),
+            pltpu.VMEM((2, cap, 2, 2, 3 * size, size), F32),
             pltpu.VMEM((rows, size), F32),
             pltpu.VMEM((rows // 2, size), F32),
             pltpu.VMEM((chips, step, size), F32),
+            pltpu.VMEM((step, size), F32),
             pltpu.VMEM((ng, step, size), F32),
-            pltpu.VMEM((step, size), F32),
             pltpu.VMEM((rows, size), F32),
             dma((2, blocks + 2)),
             dma((2, blocks + 2)),
             dma((2, blocks)),
             dma((2, 4)),
             dma((2, 4)),
-            dma((2,)),
             dma((4,)),
             dma((chips,)),
             dma((chips,)),
@@ -497,13 +531,17 @@
             collective_id=0, has_side_effects=True, vmem_limit_bytes=48 * 1024 * 1024
         ),
     )(
-        slot_offset.reshape(cap, 2),
-        slot_count,
-        slot_count,
-        object_tiles,
-        probe_modes.reshape(planes, size, size),
-        measured.reshape(cap, size, size),
-        tables,
+        *(
+            pltpu.with_memory_space_constraint(x, pltpu.HBM)
+            for x in (
+                jnp.swapaxes(slot_offset, 2, 3),
+                slot_count,
+                object_tiles,
+                probe_modes.reshape(planes, size, size),
+                measured.reshape(cap, size, size),
+                tables,
+            )
+        ),
     )
     return grad, probe_grad.reshape(probe_modes.shape)
 

time: 87.6 us -> 73.9 us (0.84)
  local copies, waits for them, and re-layouts: 10 us -> 2.72 us
  Pallas kernels: 76.7 us -> 70.4 us
    unnamed x10 -> x2, local copies, waits for them, and re-layouts: 9.24 us -> 2.72 us
    pallas_call x1, Pallas kernels: 76.7 us -> 70.4 us  [per_device(): pl.pallas_call(body, out_shape=(pltpu.VMEM(object_tiles.shape, F32), pltp...]
where the time goes in v2:
time: 73.9 us; the launch traced here: 73.8 us
  Pallas kernels  70.4 us (95%)
  local copies, waits for them, and re-layouts  2.72 us (4%)
    pallas_call x1, Pallas kernels, per_device(): pl.pallas_call(body, out_shape=(pltpu.VMEM(object_tiles.shape, F32), pltp...  70.4 us
    unnamed x2, local copies, waits for them, and re-layouts  2.72 us

profile of v2, /device:TPU:1, one launch (start us, length us, event | category | flops | bytes accessed | tf_op | source)
XLA Modules:
  0.0 73.8 jit_solution(9398533818082084168)
XLA Ops:
  0.6 70.4 %shard_map.77 = (f32[2,2,512,512]{3,2,1,0:T(8,128)S(1)}, f32[4,128,128]{2,1,0:T(8,128)S(1)}) custom-call(s32[1,1,2,8]{3,2,1,0:T(2,128)} %bitcast.7, s32[8,32]{1,0:T(8,128)} %refs_1_.1, f32[2,2,512,512]{3,2,1,0:T(8,128)} %refs_2_.1, f32[4,128,128]{2,1,0:T(8,128)} %bitcast.6, f32[8,128,128]{2,1,0:T(8,128)} %bitcast.5, ...), custom_call_target="tpu_custom_call" | custom-call | tf_op jit(solution)/shard_map/pallas_call | solution.py:483
  71.1 2.0 %copy.10 = f32[2,2,512,512]{3,2,1,0:T(8,128)} copy(f32[2,2,512,512]{3,2,1,0:T(8,128)S(1)} %get-tuple-element.6) | data formatting | bytes 8388608
  73.1 0.7 copy.11

commit v3 on v2

--- a/solution.py
+++ b/solution.py
@@ -71,6 +71,23 @@
 
 def plus(a, b):
     return a[0] + b[0], a[1] + b[1]
+
+
+class Many:
+    def __init__(self, copies):
+        self.copies = list(copies)
+
+    def start(self):
+        for copy in self.copies:
+            copy.start()
+
+    def wait_recv(self):
+        for copy in self.copies:
+            copy.wait_recv()
+
+    def wait_send(self):
+        for copy in self.copies:
+            copy.wait_send()
 
 
 def kernel(
@@ -144,8 +161,30 @@
         )
 
     barrier = pltpu.get_barrier_semaphore()
+    greeted = [up, down, left, right]
+    greeted += [(g, 2 * lax.rem(chip + d, chips) + core) for d in range(1, chips)]
+    greeted += [(lax.rem(g + d, ng), m) for d in range(2, ng - 1)]
+    for device in greeted:
+        pl.semaphore_signal(barrier, inc=1, device_id=device, device_id_type=MESH)
+    pl.semaphore_wait(barrier, len(greeted))
+
     low, wide, edge = pl.ds(tile, size), pl.ds(0, tile), pl.ds(0, size)
     rest = pl.ds(size, tile - size)
+    rims = []
+    for s in range(2):
+        rims.append(
+            [
+                remote(object_ref.at[s, :, edge, pl.ds(j * size, size)], ext[s].at[j, :, low], in_send.at[s, j], in_recv.at[s, j], up)
+                for j in range(blocks)
+            ]
+            + [
+                remote(object_ref.at[s, :, :, edge], ext[s].at[blocks, :, wide], in_send.at[s, blocks], in_recv.at[s, blocks], left),
+                remote(ext[s].at[0, :, low], ext[s].at[blocks, :, low], in_send.at[s, blocks + 1], in_recv.at[s, blocks + 1], left),
+            ]
+        )
+        for copy in rims[s][: blocks + 1]:
+            copy.start()
+
     own_copies = [
         [
             pltpu.make_async_copy(object_ref.at[s, :, :, pl.ds(j * size, size)], ext[s].at[j, :, wide], own_sem.at[s, j])
@@ -153,11 +192,6 @@
         ]
         for s in range(2)
     ]
-    greeted = [up, down, left, right]
-    greeted += [(g, 2 * lax.rem(chip + d, chips) + core) for d in range(1, chips)]
-    greeted += [(lax.rem(g + d, ng), m) for d in range(2, ng - 1)]
-    for device in greeted:
-        pl.semaphore_signal(barrier, inc=1, device_id=device, device_id_type=MESH)
     loads = [
         pltpu.make_async_copy(src, dst, load_sem.at[n])
         for n, (src, dst) in enumerate(
@@ -173,22 +207,6 @@
     ]
     for copy in loads + own_copies[0] + own_copies[1]:
         copy.start()
-    pl.semaphore_wait(barrier, len(greeted))
-
-    rims = []
-    for s in range(2):
-        rims.append(
-            [
-                remote(object_ref.at[s, :, edge, pl.ds(j * size, size)], ext[s].at[j, :, low], in_send.at[s, j], in_recv.at[s, j], up)
-                for j in range(blocks)
-            ]
-            + [
-                remote(object_ref.at[s, :, :, edge], ext[s].at[blocks, :, wide], in_send.at[s, blocks], in_recv.at[s, blocks], left),
-                remote(ext[s].at[0, :, low], ext[s].at[blocks, :, low], in_send.at[s, blocks + 1], in_recv.at[s, blocks + 1], left),
-            ]
-        )
-        for copy in rims[s][: blocks + 1]:
-            copy.start()
 
     def place(p):
         row, col = offset_ref[0, 0, 0, p], offset_ref[0, 0, 1, p]
@@ -334,7 +352,10 @@
     for s in range(2):
         homes.append(
             (
-                remote(rim_row.at[s, :, :, rest], land_row.at[s, :, :, rest], out_send.at[s, 0], out_recv.at[s, 0], down),
+                Many(
+                    remote(rim_row.at[s, :, :, part], land_row.at[s, :, :, part], out_send.at[s, 4 + j], out_recv.at[s, 4 + j], down)
+                    for j, part in ((j, pl.ds((j + 1) * size, size)) for j in range(blocks - 1))
+                ),
                 remote(rim_row.at[s, :, :, low], land_corner.at[s], out_send.at[s, 1], out_recv.at[s, 1], right),
                 remote(rim_col.at[s], land_col.at[s], out_send.at[s, 2], out_recv.at[s, 2], right),
                 remote(rim_row.at[s, :, :, edge], land_row.at[s, :, :, edge], out_send.at[s, 3], out_recv.at[s, 3], down),
@@ -346,13 +367,13 @@
         rim_row[s, :, :, edge] += land_corner[s]
         homes[s][3].start()
 
+    assemble_low(1, blocks)
+    homes[1][1].start()
+    assemble_many(1, blocks, assemble_wide)
+    homes[1][2].start()
     assemble_many(1, blocks - 1, lambda s, t: assemble_low(s, t + 1))
     homes[1][0].start()
-    assemble_low(1, blocks)
-    homes[1][1].start()
     assemble_low(1, 0)
-    assemble_many(1, blocks, assemble_wide)
-    homes[1][2].start()
 
     probe_acc[...] = jnp.zeros(probe_acc.shape, F32)
 
@@ -385,12 +406,21 @@
 
     lax.fori_loop(0, cap // PAIR, stage_three, 0)
 
+    def finish(s):
+        homes[s][2].wait_recv()
+        grad_ref[s, :, wide, edge] += land_col[s]
+        homes[s][0].wait_recv()
+        grad_ref[s, :, edge, rest] += land_row[s, :, :, rest]
+        homes[s][3].wait_recv()
+        grad_ref[s, :, edge, edge] += land_row[s, :, :, edge]
+
     rows = probe_acc.shape[0]
     half = rows // 2
     pair = remote(probe_acc.at[spot_of((1 - core) * half, half)], land_pair, pair_sem.at[0], pair_sem.at[1], partner)
     pair.start()
-    assemble_many(0, blocks + 1, assemble_low)
+    assemble_low(0, blocks)
     homes[0][1].start()
+    assemble_many(0, blocks, assemble_low)
     send_corner(1)
     pair.wait_recv()
     land_pair[...] += probe_acc[spot_of(core * half, half)]
@@ -407,6 +437,8 @@
         return total
 
     part = half // chips
+    for copy in homes[0][0].copies[:1]:
+        copy.start()
     copies = []
     for d in range(1, chips):
         other = lax.rem(chip + d, chips)
@@ -415,7 +447,6 @@
         copies[-1].start()
     land_plane[chip] = land_pair[spot_of(chip * part, part)]
     assemble_many(0, blocks, assemble_wide)
-    homes[0][2].start()
     part_sum[...] = added(land_plane, chips, copies)
     land_z[g] = part_sum[...]
     copies = []
@@ -423,10 +454,13 @@
         to = (lax.rem(g + d, ng), m)
         copies.append(remote(part_sum, land_z.at[g], z_send.at[d], z_recv.at[d], to))
         copies[-1].start()
-    homes[0][0].start()
+    for copy in homes[0][0].copies[1:]:
+        copy.start()
+    homes[0][2].start()
     send_corner(0)
     assemble_many(1, blocks * blocks, assemble_own)
     assemble_many(0, blocks * blocks, assemble_own)
+    finish(1)
     positions = jnp.sum(counts_ref[...].astype(F32), keepdims=True)
     spot = spot_of(core * half + chip * part, part)
     probe_sum[spot] = added(land_z, ng, copies) / jnp.sqrt(positions)
@@ -436,13 +470,6 @@
         copies.append(remote(probe_sum.at[spot], probe_sum.at[spot], back_send.at[d], back_recv.at[d], to))
         copies[-1].start()
 
-    def finish(s):
-        for n in (0, 2, 3):
-            homes[s][n].wait_recv()
-        grad_ref[s, :, pl.ds(0, size), wide] += land_row[s]
-        grad_ref[s, :, wide, pl.ds(0, size)] += land_col[s]
-
-    finish(1)
     for copy in copies:
         copy.wait_recv()
     sent.extend(copies)
@@ -517,8 +544,8 @@
             dma((2, blocks + 2)),
             dma((2, blocks + 2)),
             dma((2, blocks)),
-            dma((2, 4)),
-            dma((2, 4)),
+            dma((2, 3 + blocks)),
+            dma((2, 3 + blocks)),
             dma((4,)),
             dma((chips,)),
             dma((chips,)),

time: 73.9 us -> 71.8 us (0.972)
  Pallas kernels: 70.4 us -> 68.3 us
    pallas_call x1, Pallas kernels: 70.4 us -> 68.3 us  [per_device(): pl.pallas_call(body, out_shape=(pltpu.VMEM(object_tiles.shape, F32), pltp...]
where the time goes in v3:
time: 71.8 us; the launch traced here: 71.7 us
  Pallas kernels  68.3 us (95%)
  local copies, waits for them, and re-layouts  2.72 us (4%)
    pallas_call x1, Pallas kernels, per_device(): pl.pallas_call(body, out_shape=(pltpu.VMEM(object_tiles.shape, F32), pltp...  68.3 us
    unnamed x2, local copies, waits for them, and re-layouts  2.72 us

profile of v3, /device:TPU:1, one launch (start us, length us, event | category | flops | bytes accessed | tf_op | source)
XLA Modules:
  0.0 71.7 jit_solution(2175097720554810081)
XLA Ops:
  0.6 68.3 %shard_map.77 = (f32[2,2,512,512]{3,2,1,0:T(8,128)S(1)}, f32[4,128,128]{2,1,0:T(8,128)S(1)}) custom-call(s32[1,1,2,8]{3,2,1,0:T(2,128)} %bitcast.7, s32[8,32]{1,0:T(8,128)} %refs_1_.1, f32[2,2,512,512]{3,2,1,0:T(8,128)} %refs_2_.1, f32[4,128,128]{2,1,0:T(8,128)} %bitcast.6, f32[8,128,128]{2,1,0:T(8,128)} %bitcast.5, ...), custom_call_target="tpu_custom_call" | custom-call | tf_op jit(solution)/shard_map/pallas_call | solution.py:510
  69.0 2.0 %copy.10 = f32[2,2,512,512]{3,2,1,0:T(8,128)} copy(f32[2,2,512,512]{3,2,1,0:T(8,128)S(1)} %get-tuple-element.6) | data formatting | bytes 8388608
  71.0 0.7 copy.11

commit v4 on v3

--- a/solution.py
+++ b/solution.py
@@ -77,6 +77,9 @@
     def __init__(self, copies):
         self.copies = list(copies)
 
+    def __getitem__(self, key):
+        return Many(self.copies[key])
+
     def start(self):
         for copy in self.copies:
             copy.start()
@@ -88,6 +91,20 @@
     def wait_send(self):
         for copy in self.copies:
             copy.wait_send()
+
+
+class Bounded:
+    def __init__(self, copy, sends, takes):
+        self.copy, self.sends, self.takes = copy, sends, takes
+
+    def start(self):
+        pl.when(self.sends)(self.copy.start)
+
+    def wait_recv(self):
+        pl.when(self.takes)(self.copy.wait_recv)
+
+    def wait_send(self):
+        pl.when(self.sends)(self.copy.wait_send)
 
 
 def kernel(
@@ -349,28 +366,43 @@
     lax.fori_loop(0, cap // PAIR, stage_two, 0)
 
     homes = []
+    takes_rows, takes_cols = g > 0, m > 0
+
+    def home_down(*args):
+        return Bounded(remote(*args, down), g < ng - 1, takes_rows)
+
+    def home_right(*args):
+        return Bounded(remote(*args, right), m < nm - 1, takes_cols)
+
     for s in range(2):
         homes.append(
             (
                 Many(
-                    remote(rim_row.at[s, :, :, part], land_row.at[s, :, :, part], out_send.at[s, 4 + j], out_recv.at[s, 4 + j], down)
+                    home_down(rim_row.at[s, :, :, part], land_row.at[s, :, :, part], out_send.at[s, 4 + j], out_recv.at[s, 4 + j])
                     for j, part in ((j, pl.ds((j + 1) * size, size)) for j in range(blocks - 1))
                 ),
-                remote(rim_row.at[s, :, :, low], land_corner.at[s], out_send.at[s, 1], out_recv.at[s, 1], right),
-                remote(rim_col.at[s], land_col.at[s], out_send.at[s, 2], out_recv.at[s, 2], right),
-                remote(rim_row.at[s, :, :, edge], land_row.at[s, :, :, edge], out_send.at[s, 3], out_recv.at[s, 3], down),
+                home_right(rim_row.at[s, :, :, low], land_corner.at[s], out_send.at[s, 1], out_recv.at[s, 1]),
+                Many(
+                    home_right(rim_col.at[s, n], land_col.at[s, n], out_send.at[s, 2 * n], out_recv.at[s, 2 * n])
+                    for n in range(2)
+                ),
+                home_down(rim_row.at[s, :, :, edge], land_row.at[s, :, :, edge], out_send.at[s, 3], out_recv.at[s, 3]),
             )
         )
 
     def send_corner(s):
         homes[s][1].wait_recv()
-        rim_row[s, :, :, edge] += land_corner[s]
+
+        @pl.when(takes_cols)
+        def _():
+            rim_row[s, :, :, edge] += land_corner[s]
+
         homes[s][3].start()
 
     assemble_low(1, blocks)
     homes[1][1].start()
     assemble_many(1, blocks, assemble_wide)
-    homes[1][2].start()
+    homes[1][2].copies[0].start()
     assemble_many(1, blocks - 1, lambda s, t: assemble_low(s, t + 1))
     homes[1][0].start()
     assemble_low(1, 0)
@@ -408,11 +440,22 @@
 
     def finish(s):
         homes[s][2].wait_recv()
-        grad_ref[s, :, wide, edge] += land_col[s]
+
+        @pl.when(takes_cols)
+        def _():
+            grad_ref[s, :, wide, edge] += land_col[s]
+
         homes[s][0].wait_recv()
-        grad_ref[s, :, edge, rest] += land_row[s, :, :, rest]
+
+        @pl.when(takes_rows)
+        def _():
+            grad_ref[s, :, edge, rest] += land_row[s, :, :, rest]
+
         homes[s][3].wait_recv()
-        grad_ref[s, :, edge, edge] += land_row[s, :, :, edge]
+
+        @pl.when(takes_rows)
+        def _():
+            grad_ref[s, :, edge, edge] += land_row[s, :, :, edge]
 
     rows = probe_acc.shape[0]
     half = rows // 2
@@ -437,8 +480,6 @@
         return total
 
     part = half // chips
-    for copy in homes[0][0].copies[:1]:
-        copy.start()
     copies = []
     for d in range(1, chips):
         other = lax.rem(chip + d, chips)
@@ -454,9 +495,9 @@
         to = (lax.rem(g + d, ng), m)
         copies.append(remote(part_sum, land_z.at[g], z_send.at[d], z_recv.at[d], to))
         copies[-1].start()
-    for copy in homes[0][0].copies[1:]:
-        copy.start()
-    homes[0][2].start()
+    homes[0][0].start()
+    homes[1][2].copies[1].start()
+    homes[0][2].copies[0].start()
     send_corner(0)
     assemble_many(1, blocks * blocks, assemble_own)
     assemble_many(0, blocks * blocks, assemble_own)
@@ -470,6 +511,7 @@
         copies.append(remote(probe_sum.at[spot], probe_sum.at[spot], back_send.at[d], back_recv.at[d], to))
         copies[-1].start()
 
+    homes[0][2].copies[1].start()
     for copy in copies:
         copy.wait_recv()
     sent.extend(copies)

time: 71.8 us -> 68.1 us (0.948)
  Pallas kernels: 68.3 us -> 64.6 us
    pallas_call x1, Pallas kernels: 68.3 us -> 64.6 us  [per_device(): pl.pallas_call(body, out_shape=(pltpu.VMEM(object_tiles.shape, F32), pltp...]
where the time goes in v4:
time: 68.1 us; the launch traced here: 68 us
  Pallas kernels  64.6 us (95%)
  local copies, waits for them, and re-layouts  2.72 us (4%)
    pallas_call x1, Pallas kernels, per_device(): pl.pallas_call(body, out_shape=(pltpu.VMEM(object_tiles.shape, F32), pltp...  64.6 us
    unnamed x2, local copies, waits for them, and re-layouts  2.72 us

profile of v4, /device:TPU:1, one launch (start us, length us, event | category | flops | bytes accessed | tf_op | source)
XLA Modules:
  0.0 68.0 jit_solution(16956696068644847947)
XLA Ops:
  0.6 64.6 %shard_map.77 = (f32[2,2,512,512]{3,2,1,0:T(8,128)S(1)}, f32[4,128,128]{2,1,0:T(8,128)S(1)}) custom-call(s32[1,1,2,8]{3,2,1,0:T(2,128)} %bitcast.7, s32[8,32]{1,0:T(8,128)} %refs_1_.1, f32[2,2,512,512]{3,2,1,0:T(8,128)} %refs_2_.1, f32[4,128,128]{2,1,0:T(8,128)} %bitcast.6, f32[8,128,128]{2,1,0:T(8,128)} %bitcast.5, ...), custom_call_target="tpu_custom_call" | custom-call | tf_op jit(solution)/shard_map/pallas_call | solution.py:552
  65.3 2.0 %copy.10 = f32[2,2,512,512]{3,2,1,0:T(8,128)} copy(f32[2,2,512,512]{3,2,1,0:T(8,128)S(1)} %get-tuple-element.6) | data formatting | bytes 8388608
  67.3 0.7 %copy.11 = f32[2,2,128,128]{3,2,1,0:T(8,128)} copy(f32[2,2,128,128]{3,2,1,0:T(8,128)S(1)} %bitcast.4) | data formatting | bytes 524288

commit v5 on v4

--- a/solution.py
+++ b/solution.py
@@ -399,12 +399,12 @@
 
         homes[s][3].start()
 
+    assemble_many(1, blocks - 1, lambda s, t: assemble_low(s, t + 1))
+    homes[1][0].start()
     assemble_low(1, blocks)
     homes[1][1].start()
     assemble_many(1, blocks, assemble_wide)
     homes[1][2].copies[0].start()
-    assemble_many(1, blocks - 1, lambda s, t: assemble_low(s, t + 1))
-    homes[1][0].start()
     assemble_low(1, 0)
 
     probe_acc[...] = jnp.zeros(probe_acc.shape, F32)
@@ -500,8 +500,6 @@
     homes[0][2].copies[0].start()
     send_corner(0)
     assemble_many(1, blocks * blocks, assemble_own)
-    assemble_many(0, blocks * blocks, assemble_own)
-    finish(1)
     positions = jnp.sum(counts_ref[...].astype(F32), keepdims=True)
     spot = spot_of(core * half + chip * part, part)
     probe_sum[spot] = added(land_z, ng, copies) / jnp.sqrt(positions)
@@ -512,6 +510,8 @@
         copies[-1].start()
 
     homes[0][2].copies[1].start()
+    assemble_many(0, blocks * blocks, assemble_own)
+    finish(1)
     for copy in copies:
         copy.wait_recv()
     sent.extend(copies)

time: 68.1 us -> 68.3 us (level)
  no operation moved by 1% of the time
where the time goes in v5:
time: 68.3 us; the launch traced here: 68.2 us
  Pallas kernels  64.9 us (95%)
  local copies, waits for them, and re-layouts  2.72 us (4%)
    pallas_call x1, Pallas kernels, per_device(): pl.pallas_call(body, out_shape=(pltpu.VMEM(object_tiles.shape, F32), pltp...  64.9 us
    unnamed x2, local copies, waits for them, and re-layouts  2.72 us

profile of v5, /device:TPU:1, one launch (start us, length us, event | category | flops | bytes accessed | tf_op | source)
XLA Modules:
  0.0 68.2 jit_solution(13581087574368065833)
XLA Ops:
  0.6 64.9 %shard_map.77 = (f32[2,2,512,512]{3,2,1,0:T(8,128)S(1)}, f32[4,128,128]{2,1,0:T(8,128)S(1)}) custom-call(s32[1,1,2,8]{3,2,1,0:T(2,128)} %bitcast.7, s32[8,32]{1,0:T(8,128)} %refs_1_.1, f32[2,2,512,512]{3,2,1,0:T(8,128)} %refs_2_.1, f32[4,128,128]{2,1,0:T(8,128)} %bitcast.6, f32[8,128,128]{2,1,0:T(8,128)} %bitcast.5, ...), custom_call_target="tpu_custom_call" | custom-call | tf_op jit(solution)/shard_map/pallas_call | solution.py:552
  65.5 2.0 %copy.10 = f32[2,2,512,512]{3,2,1,0:T(8,128)} copy(f32[2,2,512,512]{3,2,1,0:T(8,128)S(1)} %get-tuple-element.6) | data formatting | bytes 8388608
  67.5 0.7 %copy.11 = f32[2,2,128,128]{3,2,1,0:T(8,128)} copy(f32[2,2,128,128]{3,2,1,0:T(8,128)S(1)} %bitcast.4) | data formatting | bytes 524288
